TPU v7x, 32 devices: a whole 2x2x4 slice. The times are simulated.
32 devices in a mesh: groups: 2 (over x), expert: 16 (over z, y, core).
Axes of the slice: x: 2, y: 2, z: 4, core: 2. Of those that a mesh axis runs over, the one named last changes fastest.
Arguments:
- tokens: bfloat16 [4096, 2048], P(('groups', 'expert')), parts along dimension 0, may hold values from -12 to 12
- out_grad: bfloat16 [4096, 2048], P(('groups', 'expert')), parts along dimension 0, may hold values from -6 to 6
- cluster_ids: int32 [4096], P(('groups', 'expert')), parts along dimension 0, may hold values from 0 to 31, as said below
- routes: int32 [1024, 8], P(('groups', 'expert')), parts along dimension 0, may hold values from 0 to 15, all different within a row; in each aligned block of 32 rows (0 to 31, 32 to 63, ...) at most 32 rows name the same one
- route_weights: float32 [1024, 8], P(('groups', 'expert')), parts along dimension 0, may hold values from 0.05 to 0.5
- gate_weight: bfloat16 [16, 2048, 768], P('expert'), may hold values from -0.125 to 0.125
- up_weight: bfloat16 [16, 2048, 768], P('expert'), may hold values from -0.125 to 0.125
- down_weight: bfloat16 [16, 768, 2048], P('expert'), may hold values from -0.21875 to 0.21875
Outputs:
- layer_out: float32 [4096, 2048], P(('groups', 'expert')), parts along dimension 0
- token_grad: float32 [4096, 2048], P(('groups', 'expert')), parts along dimension 0
There are 2 independent parts, one for each index of `groups`. A program takes and returns all parts, laid end to end along the dimension named above; an argument that names none is the same for every part. Nothing has to cross between parts.
Inputs may be any that keep to these rules, and one draw needn't show every extreme that they name: `cluster_ids`: within each block of 128 tokens every one of the 32 cluster numbers occurs at least once. `routes`: each row names 8 different experts. Among the 32 rows of one index of expert no expert is named more than 32 times, and in some such blocks one expert is named exactly 32 times.
All inputs are finite; a program needn't handle non-finite values.
Results may differ from a plain program's by a relative error of at most 0.0027.
Values may be sent and summed in bfloat16 or wider, within the bound.
A program may use at most 64 MiB of HBM per device.

v0:
```python
import functools
import jax
import jax.numpy as jnp
from jax import lax
from jax.experimental import pallas as pl
from jax.experimental.pallas import tpu as pltpu
from jax.sharding import PartitionSpec as P


def expert_forward(inputs, gate_mat, up_mat, down_mat):
    gate_act = jnp.dot(inputs, gate_mat, preferred_element_type=jnp.float32)
    up_act = jnp.dot(inputs, up_mat, preferred_element_type=jnp.float32)
    sigmoid_gate = jax.nn.sigmoid(gate_act)
    hidden = (gate_act * sigmoid_gate * up_act).astype(jnp.bfloat16)
    output = jnp.dot(hidden, down_mat, preferred_element_type=jnp.float32).astype(jnp.bfloat16)
    return (output, gate_act, up_act)


def expert_backward(incoming, gate_act, up_act, gate_mat, up_mat, down_mat):
    against = (((1,), (1,)), ((), ()))
    hidden_grad = lax.dot_general(incoming, down_mat, against, preferred_element_type=jnp.float32)
    sigmoid_gate = jax.nn.sigmoid(gate_act)
    gate_grad = (
        hidden_grad * up_act * sigmoid_gate * (1.0 + gate_act * (1.0 - sigmoid_gate))
    ).astype(jnp.bfloat16)
    up_grad = (hidden_grad * gate_act * sigmoid_gate).astype(jnp.bfloat16)
    summed = lax.dot_general(gate_grad, gate_mat, against, preferred_element_type=jnp.float32)
    summed = summed + lax.dot_general(up_grad, up_mat, against, preferred_element_type=jnp.float32)
    return summed.astype(jnp.bfloat16)


def per_device(
    tokens, out_grad, cluster_ids, routes, route_weights, gate_weight, up_weight, down_weight
):
    model_width = tokens.shape[1]
    cent_rows = routes.shape[0]
    fanout = routes.shape[1]
    experts = lax.axis_size("expert")
    capacity = min(cent_rows, 2 * cent_rows * fanout // experts)
    member = (cluster_ids[:, None] == jnp.arange(cent_rows, dtype=jnp.int32)[None, :]).astype(
        jnp.bfloat16
    )
    counts = jnp.sum(member.astype(jnp.float32), axis=0)
    contract = (((0,), (0,)), ((), ()))
    centroid = (
        lax.dot_general(member, tokens, contract, preferred_element_type=jnp.float32)
        / counts[:, None]
    )
    grad_sum = lax.dot_general(member, out_grad, contract, preferred_element_type=jnp.float32)
    pair_ids = routes.reshape(-1)
    matches = (pair_ids[:, None] == jnp.arange(experts, dtype=jnp.int32)[None, :]).astype(jnp.int32)
    earlier = jnp.cumsum(matches, axis=0) - matches
    position = jnp.sum(earlier * matches, axis=1)
    slot_of = (pair_ids * capacity + position).reshape(cent_rows, fanout)
    slot_range = jnp.arange(experts * capacity, dtype=jnp.int32)
    placing = jnp.any(slot_of[None, :, :] == slot_range[:, None, None], axis=2).astype(jnp.bfloat16)
    send_cent = jnp.dot(placing, centroid.astype(jnp.bfloat16), preferred_element_type=jnp.float32)
    send_cent = send_cent.astype(jnp.bfloat16).reshape(experts, capacity, model_width)
    send_grad = jnp.dot(placing, grad_sum.astype(jnp.bfloat16), preferred_element_type=jnp.float32)
    send_grad = send_grad.astype(jnp.bfloat16).reshape(experts, capacity, model_width)
    gate_mat = gate_weight[0]
    up_mat = up_weight[0]
    down_mat = down_weight[0]
    arrived = lax.all_to_all(send_cent, "expert", split_axis=0, concat_axis=0, tiled=True)
    output, gate_act, up_act = expert_forward(
        arrived.reshape(-1, model_width), gate_mat, up_mat, down_mat
    )
    results = lax.all_to_all(
        output.reshape(experts, capacity, model_width),
        "expert",
        split_axis=0,
        concat_axis=0,
        tiled=True,
    )
    arrived_grad = lax.all_to_all(send_grad, "expert", split_axis=0, concat_axis=0, tiled=True)
    input_grad = expert_backward(
        arrived_grad.reshape(-1, model_width), gate_act, up_act, gate_mat, up_mat, down_mat
    )
    results_grad = lax.all_to_all(
        input_grad.reshape(experts, capacity, model_width),
        "expert",
        split_axis=0,
        concat_axis=0,
        tiled=True,
    )
    returned = results.reshape(-1, model_width)[slot_of]
    returned_grad = results_grad.reshape(-1, model_width)[slot_of]
    combined = jnp.sum(route_weights[:, :, None] * returned.astype(jnp.float32), axis=1)
    centroid_grad = (
        jnp.sum(route_weights[:, :, None] * returned_grad.astype(jnp.float32), axis=1) - grad_sum
    )
    layer_out = tokens.astype(jnp.float32) + jnp.take(combined - centroid, cluster_ids, axis=0)
    token_grad = out_grad.astype(jnp.float32) + jnp.take(
        centroid_grad / counts[:, None], cluster_ids, axis=0
    )
    return (layer_out, token_grad)


AGAINST = (((1,), (1,)), ((), ()))


def ring_layout(ring):
    half = ring // 2
    places = {0: 0}
    for hop in range(1, half):
        places[hop] = 2 * hop - 1
        places[-hop] = 2 * hop
    places[half] = ring - 1
    places[-half] = ring - 1
    return places


def exchange_kernel(
    experts,
    ids_ref,
    tokens_ref,
    out_grad_ref,
    routes_ref,
    route_weights_ref,
    gate_ref,
    up_ref,
    down_ref,
    delta_ref,
    delta_grad_ref,
    cent_all,
    grad_all,
    gate_up,
    down,
    gate_up_turned,
    down_turned,
    hidden,
    hidden_grads,
    part_cent,
    part_grad,
    twin_cent,
    twin_grad,
    outgoing,
    incoming,
    centroid_keep,
    grad_keep,
    weight_sems,
    gather_send,
    gather_recv,
    share_send,
    share_recv,
    twin_send,
    twin_recv,
    ring_send,
    ring_recv,
):
    fanout, rows = routes_ref.shape
    width = tokens_ref.shape[1]
    hidden_width = down.shape[0]
    ring = experts // 2
    half = ring // 2
    places = ring_layout(ring)
    gathered = (cent_all, grad_all)
    parts = (part_cent, part_grad)
    twins = (twin_cent, twin_grad)

    me = lax.axis_index("expert")
    core = me % 2
    chip = me // 2
    column = chip % 2
    height = chip // 2
    spot = height + column * (ring - 1 - 2 * height)

    def device_at(position):
        side = position // half
        level = position + side * (ring - 1 - 2 * position)
        return (level * 2 + side) * 2 + core

    neighbour = (device_at((spot + 1) % ring), device_at((spot + ring - 1) % ring))
    twin = chip * 2 + (1 - core)

    weight_copies = [
        pltpu.make_async_copy(
            gate_ref.at[0], gate_up.at[:, pl.ds(0, hidden_width)], weight_sems.at[0]
        ),
        pltpu.make_async_copy(
            up_ref.at[0], gate_up.at[:, pl.ds(hidden_width, hidden_width)], weight_sems.at[1]
        ),
        pltpu.make_async_copy(down_ref.at[0], down, weight_sems.at[2]),
    ]
    for number in (2, 0, 1):
        weight_copies[number].start()

    barrier = pltpu.get_barrier_semaphore()
    for other in (neighbour[0], neighbour[1], twin):
        pl.semaphore_signal(
            barrier, inc=1, device_id={"expert": other}, device_id_type=pl.DeviceIdType.MESH
        )

    def block(distance, which):
        return pl.ds((places[distance] * 2 + which) * rows, rows)

    members = (
        lax.broadcasted_iota(jnp.int32, (rows, ids_ref.shape[1]), 0) == ids_ref[...]
    ).astype(jnp.float32)
    counts = jnp.sum(members, axis=1, keepdims=True)
    members = members.astype(jnp.bfloat16)
    centroid = jnp.dot(members, tokens_ref[...], preferred_element_type=jnp.float32) / counts
    grad_sum = jnp.dot(members, out_grad_ref[...], preferred_element_type=jnp.float32)
    centroid_keep[...] = centroid
    grad_keep[...] = grad_sum
    cent_all[block(0, 0), pl.ds(0, width)] = centroid.astype(jnp.bfloat16)
    grad_all[block(0, 0), :] = grad_sum.astype(jnp.bfloat16)

    lanes = lax.broadcasted_iota(jnp.int32, (128, rows), 0)
    spread = jnp.zeros((128, rows), jnp.float32)
    for k in range(fanout):
        spread = spread + jnp.where(
            lanes % experts == routes_ref[k : k + 1, :], route_weights_ref[k : k + 1, :], 0.0
        )
    high = spread.astype(jnp.bfloat16).astype(jnp.float32)
    middle = (spread - high).astype(jnp.bfloat16).astype(jnp.float32)
    low = spread - high - middle
    pieces = jnp.where(lanes < experts, high, jnp.where(lanes < 2 * experts, middle, low))
    same = lax.broadcasted_iota(jnp.int32, (rows, rows), 0) == lax.broadcasted_iota(
        jnp.int32, (rows, rows), 1
    )
    pieces = lax.dot_general(
        same.astype(jnp.bfloat16),
        pieces.astype(jnp.bfloat16),
        AGAINST,
        preferred_element_type=jnp.float32,
    )
    cent_all[block(0, 0), pl.ds(width, 128)] = pieces.astype(jnp.bfloat16)

    def remote(source, target, send, recv, other):
        return pltpu.make_async_remote_copy(
            src_ref=source,
            dst_ref=target,
            send_sem=send,
            recv_sem=recv,
            device_id={"expert": other},
            device_id_type=pl.DeviceIdType.MESH,
        )

    def signed(way, distance):
        return -distance if way == 0 else distance

    def hops_of(kind, way):
        return half if kind == way else half - 1

    def gather_copy(kind, way, hop):
        return remote(
            gathered[kind].at[block(signed(way, hop - 1), 0), :],
            gathered[kind].at[block(signed(way, hop), 0), :],
            gather_send.at[kind, way, hop - 1],
            gather_recv.at[kind, way, hop - 1],
            neighbour[way],
        )

    def share_copy(kind, distance):
        return remote(
            gathered[kind].at[block(distance, 0), :],
            gathered[kind].at[block(distance, 1), :],
            share_send.at[kind, places[distance]],
            share_recv.at[kind, places[distance]],
            twin,
        )

    def twin_copy(kind, distance):
        return remote(
            parts[kind].at[block(distance, 1), :],
            twins[kind].at[pl.ds(places[distance] * rows, rows), :],
            twin_send.at[kind, places[distance]],
            twin_recv.at[kind, places[distance]],
            twin,
        )

    def ring_copy(kind, way, step):
        return remote(
            outgoing.at[kind, way, step - 1],
            incoming.at[kind, way, step - 1],
            ring_send.at[kind, way, step - 1],
            ring_recv.at[kind, way, step - 1],
            neighbour[way],
        )

    started = []

    def start(copy):
        copy.start()
        started.append(copy)

    pl.semaphore_wait(barrier, 3)
    for way in range(2):
        for kind in range(2):
            start(gather_copy(kind, way, 1))
    for kind in range(2):
        start(share_copy(kind, 0))

    tile = 256 if hidden_width % 256 == 0 else hidden_width
    wide = width // 2

    def turn(source, target, first, last):
        across = source.shape[1] // tile

        def body(r, carry):
            lines = pl.ds(pl.multiple_of(r * tile, tile), tile)
            for c in range(across):
                columns = pl.ds(c * tile, tile)
                target[columns, lines] = source[lines, columns].T
            return carry

        lax.fori_loop(first, last, body, 0)

    def first_half(low, high):
        span = pl.ds(low, high - low)
        held = pl.ds(0, high - low)

        acts = jnp.dot(
            cent_all[span, pl.ds(0, width)], gate_up[...], preferred_element_type=jnp.float32
        )
        grads = jnp.dot(grad_all[span, :], down_turned[...], preferred_element_type=jnp.float32)
        gate_act = acts[:, :hidden_width]
        up_act = acts[:, hidden_width:]
        sigmoid_gate = jax.nn.sigmoid(gate_act)
        hidden[held, :] = (gate_act * sigmoid_gate * up_act).astype(jnp.bfloat16)
        hidden_grads[held, pl.ds(0, hidden_width)] = (
            grads * up_act * sigmoid_gate * (1.0 + gate_act * (1.0 - sigmoid_gate))
        ).astype(jnp.bfloat16)
        hidden_grads[held, pl.ds(hidden_width, hidden_width)] = (
            grads * gate_act * sigmoid_gate
        ).astype(jnp.bfloat16)

    def second_half(low, high):
        span = pl.ds(low, high - low)
        held = pl.ds(0, high - low)
        pieces = cent_all[span, pl.ds(width, 128)].astype(jnp.float32)
        lanes = lax.broadcasted_iota(jnp.int32, (high - low, 128), 1)
        own = (lanes % experts == me) & (lanes < 3 * experts)
        weight = jnp.sum(jnp.where(own, pieces, 0.0), axis=1, keepdims=True)

        for t in range(2):
            columns = pl.ds(t * wide, wide)
            output = jnp.dot(hidden[held, :], down[:, columns], preferred_element_type=jnp.float32)
            output = output.astype(jnp.bfloat16).astype(jnp.float32)
            part_cent[span, columns] = output * weight
            summed = jnp.dot(
                hidden_grads[held, :],
                gate_up_turned[:, columns],
                preferred_element_type=jnp.float32,
            )
            summed = summed.astype(jnp.bfloat16).astype(jnp.float32)
            part_grad[span, columns] = summed * weight

    def contribution(kind, distance):
        twin_copy(kind, distance).wait_recv()
        return (
            parts[kind][block(distance, 0), :]
            + twins[kind][pl.ds(places[distance] * rows, rows), :]
        )

    def toward(way, distance):
        return distance if way == 0 else -distance

    def send_first(kind, way):
        total = contribution(kind, toward(way, hops_of(kind, way)))
        outgoing[kind, way, 0] = total.astype(jnp.bfloat16)
        start(ring_copy(kind, way, 1))

    def pass_on(hop, kind):
        for way in range(2):
            if hop <= hops_of(kind, way):
                gather_copy(kind, way, hop).wait_recv()
                if hop < hops_of(kind, way):
                    start(gather_copy(kind, way, hop + 1))
                start(share_copy(kind, signed(way, hop)))

    def distances_of(hop):
        if hop == 0 or hop == half:
            return (hop,)
        return (hop, -hop)

    def wait_shares(hop):
        for kind in range(2):
            for distance in distances_of(hop):
                share_copy(kind, distance).wait_recv()

    def start_twins(hop):
        for distance in distances_of(hop):
            for kind in range(2):
                start(twin_copy(kind, distance))

    bands = width // tile
    weight_copies[2].wait()
    turn(down, down_turned, 0, hidden_width // tile)
    pass_on(1, 0)
    weight_copies[0].wait()
    weight_copies[1].wait()
    turn(gate_up, gate_up_turned, 0, bands // 2)
    pass_on(1, 1)
    turn(gate_up, gate_up_turned, bands // 2, bands)
    low = 0
    for hop in range(1, half + 1):
        included = (0, 1) if hop == 1 else (hop,)
        high = low + sum(len(distances_of(each)) for each in included) * 2 * rows
        if hop < half:
            pass_on(hop + 1, 0)
        for each in included:
            wait_shares(each)
        first_half(low, high)
        if hop < half:
            pass_on(hop + 1, 1)
        else:
            for kind in range(2):
                send_first(kind, 1 - kind)
        second_half(low, high)
        for each in included:
            start_twins(each)
        low = high

    for kind in range(2):
        send_first(kind, kind)
    totals = [contribution(kind, 0) for kind in range(2)]
    delta_ref[...] = totals[0] - centroid_keep[...]
    delta_grad_ref[...] = totals[1] - grad_keep[...]
    for step in range(1, half + 1):
        for kind in range(2):
            for way in (1 - kind, kind):
                hops = hops_of(kind, way)
                if step > hops:
                    continue
                ring_copy(kind, way, step).wait_recv()
                arrived = incoming[kind, way, step - 1].astype(jnp.float32)
                if step < hops:
                    total = arrived + contribution(kind, toward(way, hops - step))
                    outgoing[kind, way, step] = total.astype(jnp.bfloat16)
                    start(ring_copy(kind, way, step + 1))
                elif kind == 0:
                    delta_ref[...] += arrived
                else:
                    delta_grad_ref[...] += arrived
    delta_grad_ref[...] = delta_grad_ref[...] / counts
    for copy in started:
        copy.wait_send()


def decode_kernel(ids_ref, tokens_ref, out_grad_ref, delta_ref, delta_grad_ref, out_ref, grad_ref):
    rows = delta_ref.shape[0]
    lines = lax.broadcasted_iota(jnp.int32, (3 * rows, ids_ref.shape[1]), 0)
    members = (lines % rows == ids_ref[...]).astype(jnp.bfloat16)
    contract = (((0,), (0,)), ((), ()))

    def spread(table):
        high = table.astype(jnp.bfloat16)
        rest = table - high.astype(jnp.float32)
        middle = rest.astype(jnp.bfloat16)
        low = (rest - middle.astype(jnp.float32)).astype(jnp.bfloat16)
        stacked = jnp.concatenate([high, middle, low], axis=0)
        return lax.dot_general(members, stacked, contract, preferred_element_type=jnp.float32)

    out_ref[...] = tokens_ref[...].astype(jnp.float32) + spread(delta_ref[...])
    grad_ref[...] = out_grad_ref[...].astype(jnp.float32) + spread(delta_grad_ref[...])


def ring_per_device(
    tokens, out_grad, cluster_ids, routes, route_weights, gate_weight, up_weight, down_weight
):
    experts = lax.axis_size("expert")
    rows = routes.shape[0]
    count, width = tokens.shape
    hidden_width = gate_weight.shape[2]
    ring = experts // 2
    half = ring // 2
    held = experts * rows
    ids = cluster_ids.reshape(1, count)
    vmem = pl.BlockSpec(memory_space=pltpu.VMEM)
    anywhere = pl.BlockSpec(memory_space=pl.ANY)
    table = jax.ShapeDtypeStruct((rows, width), jnp.float32)
    bf16, f32, dma = jnp.bfloat16, jnp.float32, pltpu.SemaphoreType.DMA
    delta, delta_grad = pl.pallas_call(
        functools.partial(exchange_kernel, experts),
        out_shape=(table, table),
        in_specs=[vmem] * 5 + [anywhere] * 3,
        out_specs=(vmem, vmem),
        scratch_shapes=[
            pltpu.VMEM((held, width + 128), bf16),
            pltpu.VMEM((held, width), bf16),
            pltpu.VMEM((width, 2 * hidden_width), bf16),
            pltpu.VMEM((hidden_width, width), bf16),
            pltpu.VMEM((2 * hidden_width, width), bf16),
            pltpu.VMEM((width, hidden_width), bf16),
            pltpu.VMEM((6 * rows, hidden_width), bf16),
            pltpu.VMEM((6 * rows, 2 * hidden_width), bf16),
            pltpu.VMEM((held, width), f32),
            pltpu.VMEM((held, width), f32),
            pltpu.VMEM((ring * rows, width), f32),
            pltpu.VMEM((ring * rows, width), f32),
            pltpu.VMEM((2, 2, half, rows, width), bf16),
            pltpu.VMEM((2, 2, half, rows, width), bf16),
            pltpu.VMEM((rows, width), f32),
            pltpu.VMEM((rows, width), f32),
            dma((3,)),
            dma((2, 2, half)),
            dma((2, 2, half)),
            dma((2, ring)),
            dma((2, ring)),
            dma((2, ring)),
            dma((2, ring)),
            dma((2, 2, half)),
            dma((2, 2, half)),
        ],
        compiler_params=pltpu.CompilerParams(
            collective_id=0, has_side_effects=True, vmem_limit_bytes=56 * 1024 * 1024
        ),
        cost_estimate=pl.CostEstimate(
            flops=12 * held * width * hidden_width,
            bytes_accessed=6 * width * hidden_width,
            transcendentals=held * hidden_width,
        ),
    )(ids, tokens, out_grad, routes.T, route_weights.T, gate_weight, up_weight, down_weight)
    step = 512 if width % 512 == 0 else width
    whole = pl.BlockSpec((1, count), lambda i: (0, 0))
    tall = pl.BlockSpec((count, step), lambda i: (0, i))
    short = pl.BlockSpec((rows, step), lambda i: (0, i))
    result = jax.ShapeDtypeStruct((count, width), jnp.float32)
    return pl.pallas_call(
        decode_kernel,
        grid=(width // step,),
        out_shape=(result, result),
        in_specs=[whole, tall, tall, short, short],
        out_specs=(tall, tall),
    )(ids, tokens, out_grad, delta, delta_grad)


def solution(mesh):
    placed = (
        P(("groups", "expert"), None),
        P(("groups", "expert"), None),
        P(("groups", "expert")),
        P(("groups", "expert"), None),
        P(("groups", "expert"), None),
        P("expert", None, None),
        P("expert", None, None),
        P("expert", None, None),
    )
    size = mesh.shape["expert"]
    ringed = size % 4 == 0 and 12 <= size <= 32
    return jax.shard_map(
        ring_per_device if ringed else per_device,
        mesh=mesh,
        in_specs=placed,
        out_specs=(P(("groups", "expert"), None), P(("groups", "expert"), None)),
        check_vma=False,
    )
```

profile of v0, /device:TPU:0, one launch (start us, length us, event | category | flops | bytes accessed | tf_op | source)
XLA Modules:
  0.0 65.5 jit_solution(14798556120141751888)
XLA Ops:
  0.6 60.8 %shard_map.95 = (f32[32,2048]{1,0:T(8,128)}, f32[32,2048]{1,0:T(8,128)}) custom-call(s32[1,128]{1,0:T(1,128)} %bitcast.3, bf16[128,2048]{1,0:T(8,128)(2,1)} %tokens_ref.3, bf16[128,2048]{1,0:T(8,128)(2,1)} %out_grad_ref.3, s32[8,32]{1,0:T(8,128)} %bitcast.5, f32[8,32]{1,0:T(8,128)} %bitcast.6, bf16[1,2048,768]{2,1,0:T(8,128)(2,1)} %gate_ref.1, ...), custom_call_target="tpu_custom_call" | custom-call | flops 9663676416 | bytes 9437184 | tf_op jit(solution)/shard_map/pallas_call | solution.py:475
  61.4 4.0 %shard_map.96 = (f32[128,2048]{1,0:T(8,128)}, f32[128,2048]{1,0:T(8,128)}) custom-call(s32[1,128]{1,0:T(1,128)} %bitcast.4, bf16[128,2048]{1,0:T(8,128)(2,1)} %tokens_ref.3, bf16[128,2048]{1,0:T(8,128)(2,1)} %out_grad_ref.3, f32[32,2048]{1,0:T(8,128)} %get-tuple-element.4.delta_ref, f32[32,2048]{1,0:T(8,128)} %get-tuple-element.5.delta_grad_ref), custom_call_target="tpu_custom_call" | custom-call | tf_op jit(solution)/shard_map/pallas_call | solution.py:521
where the time goes:
time: 65.7 us; the launch traced here: 65.5 us
  Pallas kernels  64.8 us (99%)
    pallas_call x1, Pallas kernels, ring_per_device(): pl.pallas_call(functools.partial(exchange_kernel, experts), out_shape=(ta...  60.8 us
    pallas_call x1, Pallas kernels, ring_per_device(): pl.pallas_call(decode_kernel, grid=(width // step,), out_shape=(result, r...  4.05 us

commit v1 on v0

--- a/solution.py
+++ b/solution.py
@@ -153,6 +153,7 @@
     hidden_width = down.shape[0]
     ring = experts // 2
     half = ring // 2
+    wide = width // 2
     places = ring_layout(ring)
     gathered = (cent_all, grad_all)
     parts = (part_cent, part_grad)
@@ -261,21 +262,22 @@
             twin,
         )
 
-    def twin_copy(kind, distance):
+    def twin_copy(kind, distance, piece):
+        columns = pl.ds(piece * wide, wide)
         return remote(
-            parts[kind].at[block(distance, 1), :],
-            twins[kind].at[pl.ds(places[distance] * rows, rows), :],
-            twin_send.at[kind, places[distance]],
-            twin_recv.at[kind, places[distance]],
+            parts[kind].at[block(distance, 1), columns],
+            twins[kind].at[pl.ds(places[distance] * rows, rows), columns],
+            twin_send.at[kind, places[distance], piece],
+            twin_recv.at[kind, places[distance], piece],
             twin,
         )
 
-    def ring_copy(kind, way, step):
+    def ring_copy(kind, way, step, piece):
         return remote(
-            outgoing.at[kind, way, step - 1],
-            incoming.at[kind, way, step - 1],
-            ring_send.at[kind, way, step - 1],
-            ring_recv.at[kind, way, step - 1],
+            outgoing.at[kind, way, step - 1, piece],
+            incoming.at[kind, way, step - 1, piece],
+            ring_send.at[kind, way, step - 1, piece],
+            ring_recv.at[kind, way, step - 1, piece],
             neighbour[way],
         )
 
@@ -293,7 +295,6 @@
         start(share_copy(kind, 0))
 
     tile = 256 if hidden_width % 256 == 0 else hidden_width
-    wide = width // 2
 
     def turn(source, target, first, last):
         across = source.shape[1] // tile
@@ -326,41 +327,38 @@
             grads * gate_act * sigmoid_gate
         ).astype(jnp.bfloat16)
 
-    def second_half(low, high):
+    def second_half(low, high, piece):
         span = pl.ds(low, high - low)
         held = pl.ds(0, high - low)
         pieces = cent_all[span, pl.ds(width, 128)].astype(jnp.float32)
         lanes = lax.broadcasted_iota(jnp.int32, (high - low, 128), 1)
         own = (lanes % experts == me) & (lanes < 3 * experts)
         weight = jnp.sum(jnp.where(own, pieces, 0.0), axis=1, keepdims=True)
-
-        for t in range(2):
-            columns = pl.ds(t * wide, wide)
-            output = jnp.dot(hidden[held, :], down[:, columns], preferred_element_type=jnp.float32)
-            output = output.astype(jnp.bfloat16).astype(jnp.float32)
-            part_cent[span, columns] = output * weight
-            summed = jnp.dot(
-                hidden_grads[held, :],
-                gate_up_turned[:, columns],
-                preferred_element_type=jnp.float32,
-            )
-            summed = summed.astype(jnp.bfloat16).astype(jnp.float32)
-            part_grad[span, columns] = summed * weight
-
-    def contribution(kind, distance):
-        twin_copy(kind, distance).wait_recv()
+        columns = pl.ds(piece * wide, wide)
+        output = jnp.dot(hidden[held, :], down[:, columns], preferred_element_type=jnp.float32)
+        output = output.astype(jnp.bfloat16).astype(jnp.float32)
+        part_cent[span, columns] = output * weight
+        summed = jnp.dot(
+            hidden_grads[held, :], gate_up_turned[:, columns], preferred_element_type=jnp.float32
+        )
+        summed = summed.astype(jnp.bfloat16).astype(jnp.float32)
+        part_grad[span, columns] = summed * weight
+
+    def contribution(kind, distance, piece):
+        columns = pl.ds(piece * wide, wide)
+        twin_copy(kind, distance, piece).wait_recv()
         return (
-            parts[kind][block(distance, 0), :]
-            + twins[kind][pl.ds(places[distance] * rows, rows), :]
+            parts[kind][block(distance, 0), columns]
+            + twins[kind][pl.ds(places[distance] * rows, rows), columns]
         )
 
     def toward(way, distance):
         return distance if way == 0 else -distance
 
-    def send_first(kind, way):
-        total = contribution(kind, toward(way, hops_of(kind, way)))
-        outgoing[kind, way, 0] = total.astype(jnp.bfloat16)
-        start(ring_copy(kind, way, 1))
+    def send_first(kind, way, piece):
+        total = contribution(kind, toward(way, hops_of(kind, way)), piece)
+        outgoing[kind, way, 0, piece] = total.astype(jnp.bfloat16)
+        start(ring_copy(kind, way, 1, piece))
 
     def pass_on(hop, kind):
         for way in range(2):
@@ -380,60 +378,69 @@
             for distance in distances_of(hop):
                 share_copy(kind, distance).wait_recv()
 
-    def start_twins(hop):
+    def start_twins(hop, piece):
         for distance in distances_of(hop):
             for kind in range(2):
-                start(twin_copy(kind, distance))
+                start(twin_copy(kind, distance, piece))
 
     bands = width // tile
+    pass_on(1, 0)
     weight_copies[2].wait()
     turn(down, down_turned, 0, hidden_width // tile)
-    pass_on(1, 0)
+    pass_on(1, 1)
     weight_copies[0].wait()
     weight_copies[1].wait()
     turn(gate_up, gate_up_turned, 0, bands // 2)
-    pass_on(1, 1)
+    pass_on(2, 0)
     turn(gate_up, gate_up_turned, bands // 2, bands)
+    pass_on(2, 1)
     low = 0
     for hop in range(1, half + 1):
         included = (0, 1) if hop == 1 else (hop,)
         high = low + sum(len(distances_of(each)) for each in included) * 2 * rows
-        if hop < half:
-            pass_on(hop + 1, 0)
         for each in included:
             wait_shares(each)
         first_half(low, high)
-        if hop < half:
-            pass_on(hop + 1, 1)
-        else:
+        if hop < half - 1:
+            pass_on(hop + 2, 0)
+        if hop == half:
             for kind in range(2):
-                send_first(kind, 1 - kind)
-        second_half(low, high)
-        for each in included:
-            start_twins(each)
+                for piece in range(2):
+                    send_first(kind, 1 - kind, piece)
+        for piece in range(2):
+            second_half(low, high, piece)
+            for each in included:
+                start_twins(each, piece)
+        if hop < half - 1:
+            pass_on(hop + 2, 1)
         low = high
 
+    for piece in range(2):
+        for kind in range(2):
+            send_first(kind, kind, piece)
+    deltas = (delta_ref, delta_grad_ref)
+    keeps = (centroid_keep, grad_keep)
     for kind in range(2):
-        send_first(kind, kind)
-    totals = [contribution(kind, 0) for kind in range(2)]
-    delta_ref[...] = totals[0] - centroid_keep[...]
-    delta_grad_ref[...] = totals[1] - grad_keep[...]
+        for piece in range(2):
+            columns = pl.ds(piece * wide, wide)
+            total = contribution(kind, 0, piece)
+            deltas[kind][:, columns] = total - keeps[kind][:, columns]
     for step in range(1, half + 1):
-        for kind in range(2):
-            for way in (1 - kind, kind):
-                hops = hops_of(kind, way)
-                if step > hops:
-                    continue
-                ring_copy(kind, way, step).wait_recv()
-                arrived = incoming[kind, way, step - 1].astype(jnp.float32)
-                if step < hops:
-                    total = arrived + contribution(kind, toward(way, hops - step))
-                    outgoing[kind, way, step] = total.astype(jnp.bfloat16)
-                    start(ring_copy(kind, way, step + 1))
-                elif kind == 0:
-                    delta_ref[...] += arrived
-                else:
-                    delta_grad_ref[...] += arrived
+        for piece in range(2):
+            columns = pl.ds(piece * wide, wide)
+            for kind in range(2):
+                for way in (1 - kind, kind):
+                    hops = hops_of(kind, way)
+                    if step > hops:
+                        continue
+                    ring_copy(kind, way, step, piece).wait_recv()
+                    arrived = incoming[kind, way, step - 1, piece].astype(jnp.float32)
+                    if step < hops:
+                        total = arrived + contribution(kind, toward(way, hops - step), piece)
+                        outgoing[kind, way, step, piece] = total.astype(jnp.bfloat16)
+                        start(ring_copy(kind, way, step + 1, piece))
+                    else:
+                        deltas[kind][:, columns] += arrived
     delta_grad_ref[...] = delta_grad_ref[...] / counts
     for copy in started:
         copy.wait_send()
@@ -490,8 +497,8 @@
             pltpu.VMEM((held, width), f32),
             pltpu.VMEM((ring * rows, width), f32),
             pltpu.VMEM((ring * rows, width), f32),
-            pltpu.VMEM((2, 2, half, rows, width), bf16),
-            pltpu.VMEM((2, 2, half, rows, width), bf16),
+            pltpu.VMEM((2, 2, half, 2, rows, width // 2), bf16),
+            pltpu.VMEM((2, 2, half, 2, rows, width // 2), bf16),
             pltpu.VMEM((rows, width), f32),
             pltpu.VMEM((rows, width), f32),
             dma((3,)),
@@ -499,10 +506,10 @@
             dma((2, 2, half)),
             dma((2, ring)),
             dma((2, ring)),
-            dma((2, ring)),
-            dma((2, ring)),
-            dma((2, 2, half)),
-            dma((2, 2, half)),
+            dma((2, ring, 2)),
+            dma((2, ring, 2)),
+            dma((2, 2, half, 2)),
+            dma((2, 2, half, 2)),
         ],
         compiler_params=pltpu.CompilerParams(
             collective_id=0, has_side_effects=True, vmem_limit_bytes=56 * 1024 * 1024
@@ -513,17 +520,12 @@
             transcendentals=held * hidden_width,
         ),
     )(ids, tokens, out_grad, routes.T, route_weights.T, gate_weight, up_weight, down_weight)
-    step = 512 if width % 512 == 0 else width
-    whole = pl.BlockSpec((1, count), lambda i: (0, 0))
-    tall = pl.BlockSpec((count, step), lambda i: (0, i))
-    short = pl.BlockSpec((rows, step), lambda i: (0, i))
     result = jax.ShapeDtypeStruct((count, width), jnp.float32)
     return pl.pallas_call(
         decode_kernel,
-        grid=(width // step,),
         out_shape=(result, result),
-        in_specs=[whole, tall, tall, short, short],
-        out_specs=(tall, tall),
+        in_specs=[vmem] * 5,
+        out_specs=(vmem, vmem),
     )(ids, tokens, out_grad, delta, delta_grad)
 
 

time: 65.7 us -> 63.6 us (0.968)
  Pallas kernels: 64.8 us -> 62.8 us
    pallas_call x1, Pallas kernels: 4.05 us -> 3.01 us  [ring_per_device(): pl.pallas_call(decode_kernel, out_shape=(result, result), in_specs=[vmem]...]
    pallas_call x1, Pallas kernels: 60.8 us -> 59.8 us  [ring_per_device(): pl.pallas_call(functools.partial(exchange_kernel, experts), out_shape=(ta...]
where the time goes in v1:
time: 63.6 us; the launch traced here: 63.4 us
  Pallas kernels  62.8 us (99%)
  between operations  0.64 us (1%)
    pallas_call x1, Pallas kernels, ring_per_device(): pl.pallas_call(functools.partial(exchange_kernel, experts), out_shape=(ta...  59.8 us
    pallas_call x1, Pallas kernels, ring_per_device(): pl.pallas_call(decode_kernel, out_shape=(result, result), in_specs=[vmem]...  3.01 us

profile of v1, /device:TPU:0, one launch (start us, length us, event | category | flops | bytes accessed | tf_op | source)
XLA Modules:
  0.0 63.4 jit_solution(3843404317215998561)
XLA Ops:
  0.6 59.8 %shard_map.95 = (f32[32,2048]{1,0:T(8,128)}, f32[32,2048]{1,0:T(8,128)}) custom-call(s32[1,128]{1,0:T(1,128)} %bitcast.3, bf16[128,2048]{1,0:T(8,128)(2,1)} %tokens_ref.3, bf16[128,2048]{1,0:T(8,128)(2,1)} %out_grad_ref.3, s32[8,32]{1,0:T(8,128)} %bitcast.5, f32[8,32]{1,0:T(8,128)} %bitcast.6, bf16[1,2048,768]{2,1,0:T(8,128)(2,1)} %gate_ref.1, ...), custom_call_target="tpu_custom_call" | custom-call | flops 9663676416 | bytes 9437184 | tf_op jit(solution)/shard_map/pallas_call | solution.py:482
  60.4 3.0 %shard_map.96 = (f32[128,2048]{1,0:T(8,128)}, f32[128,2048]{1,0:T(8,128)}) custom-call(s32[1,128]{1,0:T(1,128)} %bitcast.4, bf16[128,2048]{1,0:T(8,128)(2,1)} %tokens_ref.3, bf16[128,2048]{1,0:T(8,128)(2,1)} %out_grad_ref.3, f32[32,2048]{1,0:T(8,128)} %get-tuple-element.4.delta_ref, f32[32,2048]{1,0:T(8,128)} %get-tuple-element.5.delta_grad_ref), custom_call_target="tpu_custom_call" | custom-call | tf_op jit(solution)/shard_map/pallas_call | solution.py:524
